TPU v7x, 256 devices: a whole 4x4x8 slice. The times are simulated.
256 devices in a mesh: gx: 8 (over z), gy: 4 (over y), gz: 8 (over x, core).
Axes of the slice: x: 4, y: 4, z: 8, core: 2. Of those that a mesh axis runs over, the one named last changes fastest.
Arguments:
- adjoint_rhs: float32 [8, 4, 8, 8, 1024], P('gx', 'gy', 'gz'), may hold values from -120 to 120
- dual_operator: float32 [8, 4, 8, 1024, 1024], P('gx', 'gy', 'gz'), may hold values from -0.5 to 1.5, as said below
- dirichlet: float32 [8, 4, 8, 1024, 1024], P('gx', 'gy', 'gz'), may hold values from -0.5 to 2.5, as said below
- geneo_modes: float32 [8, 4, 8, 32, 1024], P('gx', 'gy', 'gz'), may hold values from -0.1875 to 0.1875
- coarse_inverse: float32 [8, 4, 8, 32, 8192], P('gx', 'gy', 'gz'), may hold values from -0.5 to 1.5, as said below
- partner_slot: int32 [8, 4, 8, 1024], P('gx', 'gy', 'gz'), may hold values from 0 to 1023, as said below
- jump_sign: int32 [8, 4, 8, 1024], P('gx', 'gy', 'gz'), may hold values from -1 to 1, as said below
- mode_count: int32 [8, 4, 8], P('gx', 'gy', 'gz'), may hold values from 8 to 32
Outputs:
- dual_solution: float32 [8, 4, 8, 8, 1024], P('gx', 'gy', 'gz')
- interface_force: float32 [8, 4, 8, 8, 1024], P('gx', 'gy', 'gz')
Inputs may be any that keep to these rules, and one draw needn't show every extreme that they name: `dual_operator`: symmetric positive definite. `dirichlet`: symmetric positive definite. `coarse_inverse`: the whole 8192-order coarse inverse, rows and columns ordered as the coefficients, is symmetric positive definite. `partner_slot`: for a paired slot of block d, the partner slot lies in the neighbour's block of direction -d, and the neighbour's partner of it is this slot again. On unpaired slots the value is the slot's own index. `jump_sign`: A paired slot and its partner have opposite signs.
All inputs are finite; a program needn't handle non-finite values.
Results may differ from a plain program's by a relative error of at most 0.0003.
Values sent between devices are 32-bit elements; how exact they have to be, the bound alone decides.
A program may use at most 64 MiB of HBM per device.

v0:
```python
import jax
import jax.numpy as jnp
from jax import lax
from jax.sharding import PartitionSpec as P

FACE_SLOTS = 144
EDGE_SLOTS = 12
CORNER_SLOTS = 2
DUAL_STEPS = 3


def from_behind(block, axis, distance):
    devices = range(lax.axis_size(axis))
    route = [(i - distance, i) for i in devices if i - distance in devices]
    return lax.ppermute(block, axis, route)


def block_list():
    blocks = []
    cursor = 0
    for shift_first in (-1, 0, 1):
        for shift_second in (-1, 0, 1):
            for shift_third in (-1, 0, 1):
                nonzero = abs(shift_first) + abs(shift_second) + abs(shift_third)
                if nonzero == 0:
                    continue
                extent = (
                    FACE_SLOTS if nonzero == 1 else EDGE_SLOTS if nonzero == 2 else CORNER_SLOTS
                )
                blocks.append(((shift_first, shift_second, shift_third), cursor, extent))
                cursor += extent
    return blocks


def product(former, latter):
    return jnp.dot(
        former, latter, precision=lax.Precision.HIGHEST, preferred_element_type=jnp.float32
    )


def contract_last(former, latter):
    return lax.dot_general(
        former,
        latter,
        (((1,), (1,)), ((), ())),
        precision=lax.Precision.HIGHEST,
        preferred_element_type=jnp.float32,
    )


def section_hop(bundle, axis_number, toward):
    if axis_number == 0:
        return from_behind(bundle, "gx", toward)
    if axis_number == 1:
        return from_behind(bundle, "gy", toward)
    return from_behind(bundle, "gz", toward)


def neighbour_values(values):
    blocks = block_list()
    pieces = {}
    for direction, cursor, extent in blocks:
        pieces[direction] = values[:, cursor : cursor + extent]
    for axis_number in (0, 1, 2):
        for toward in (1, -1):
            chosen = [record for record in blocks if record[0][axis_number] == toward]
            bundle = jnp.concatenate([pieces[record[0]] for record in chosen], axis=1)
            arrived = section_hop(bundle, axis_number, toward)
            cursor = 0
            for record in chosen:
                pieces[record[0]] = arrived[:, cursor : cursor + record[2]]
                cursor += record[2]
    return jnp.concatenate([pieces[record[0]] for record in blocks], axis=1)


def paired_mask():
    places = (lax.axis_index("gx"), lax.axis_index("gy"), lax.axis_index("gz"))
    extents = (lax.axis_size("gx"), lax.axis_size("gy"), lax.axis_size("gz"))
    pieces = []
    for direction, cursor, extent in block_list():
        inside = jnp.array(True)
        for axis_number in (0, 1, 2):
            target = places[axis_number] + direction[axis_number]
            inside = inside & (target >= 0) & (target < extents[axis_number])
        pieces.append(jnp.broadcast_to(inside.astype(jnp.float32), (extent,)))
    return jnp.concatenate(pieces)


def body(
    adjoint_rhs,
    dual_operator,
    dirichlet,
    geneo_modes,
    coarse_inverse,
    partner_slot,
    jump_sign,
    mode_count,
):
    load_count = adjoint_rhs.shape[3]
    dual_order = adjoint_rhs.shape[4]
    right_side = adjoint_rhs.reshape(load_count, dual_order)
    operator_block = dual_operator.reshape(dual_order, dual_order)
    dirichlet_block = dirichlet.reshape(dual_order, dual_order)
    mode_total = geneo_modes.shape[3]
    mode_table = geneo_modes.reshape(mode_total, dual_order)
    coarse_rows = coarse_inverse.reshape(mode_total, coarse_inverse.shape[4])
    partner = partner_slot.reshape(dual_order)
    sign_values = jump_sign.reshape(dual_order).astype(jnp.float32)
    in_use = (jnp.arange(mode_total) < mode_count.reshape(())).astype(jnp.float32)
    paired = paired_mask()
    weight = 1.0 - 0.5 * paired

    def assemble(values):
        arrived = neighbour_values(values)
        return values + paired * jnp.take(arrived, partner, axis=1)

    def coefficients(current):
        return contract_last(current, mode_table) * in_use

    def precondition(current, coeff_all):
        scaled = weight * sign_values
        local_term = scaled * product(scaled * current, dirichlet_block)
        coarse = contract_last(coeff_all, coarse_rows) * in_use
        return assemble(local_term + product(coarse, mode_table))

    def global_inner(former, latter):
        return lax.psum(jnp.sum(weight * former * latter, axis=1), ("gx", "gy", "gz"))

    solution = jnp.zeros_like(right_side)
    residual = right_side
    coeff_all = lax.all_gather(coefficients(residual), ("gx", "gy", "gz"), axis=1, tiled=True)
    preconditioned = precondition(residual, coeff_all)
    energy = global_inner(residual, preconditioned)
    direction = preconditioned
    for step_number in range(DUAL_STEPS):
        mapped = assemble(sign_values * product(sign_values * direction, operator_block))
        partial_curve = jnp.sum(weight * direction * mapped, axis=1)
        curvature = lax.psum(partial_curve, ("gx", "gy", "gz"))
        step_size = (energy / curvature)[:, None]
        solution = solution + step_size * direction
        residual = residual - step_size * mapped
        coeff_all = lax.all_gather(coefficients(residual), ("gx", "gy", "gz"), axis=1, tiled=True)
        preconditioned = precondition(residual, coeff_all)
        if step_number + 1 < DUAL_STEPS:
            energy_next = global_inner(residual, preconditioned)
            direction = preconditioned + (energy_next / energy)[:, None] * direction
            energy = energy_next
    return (solution.reshape(adjoint_rhs.shape), preconditioned.reshape(adjoint_rhs.shape))


def solution(mesh):
    placed = (
        P("gx", "gy", "gz", None, None),
        P("gx", "gy", "gz", None, None),
        P("gx", "gy", "gz", None, None),
        P("gx", "gy", "gz", None, None),
        P("gx", "gy", "gz", None, None),
        P("gx", "gy", "gz", None),
        P("gx", "gy", "gz", None),
        P("gx", "gy", "gz"),
    )
    return jax.shard_map(
        body,
        mesh=mesh,
        in_specs=placed,
        out_specs=(P("gx", "gy", "gz", None, None), P("gx", "gy", "gz", None, None)),
        check_vma=False,
    )
```

profile of v0, /device:TPU:1, one launch (start us, length us, event | category | flops | bytes accessed | tf_op | source)
XLA Modules:
  0.0 867.6 jit_solution(3439256136431647353)
XLA Ops:
  3.4 67.6 %all-gather = f32[256,32,8]{1,2,0:T(8,128)S(1)} all-gather(f32[1,32,8]{1,2,0:T(8,128)S(1)} %fusion.50), channel_id=1, replica_groups=mesh['gx'=8,'gy'=4,'gz'=8] {'gx','gy','gz'}, dimensions={0}, use_global_device_ids=true | all-gather | bytes 263168 | tf_op jit(solution)/shard_map/all_gather | solution.py:131
  73.3 4.3 fusion.17
  78.9 4.0 collective-permute-start.1
  103.8 4.3 fusion.38
  109.6 4.5 collective-permute-start.7
  123.1 4.2 collective-permute-start.11
  136.3 77.1 %all-reduce = (f32[8]{0:T(128)S(1)}, f32[8]{0:T(128)S(1)}) all-reduce(f32[8]{0:T(128)S(1)} %get-tuple-element.4, f32[8]{0:T(128)S(1)} %get-tuple-element.3), channel_id=1, replica_groups=mesh['gx'=8,'gy'=4,'gz'=8] {'gx','gy','gz'}, use_global_device_ids=true, to_apply=%region_1.3 | all-reduce | flops 16 | bytes 128 | tf_op jit(solution)/shard_map/psum | solution.py:127
  213.7 60.7 %all-gather.1 = f32[256,32,8]{1,2,0:T(8,128)S(1)} all-gather(f32[1,32,8]{1,2,0:T(8,128)S(1)} %fusion.49), channel_id=1, replica_groups=mesh['gx'=8,'gy'=4,'gz'=8] {'gx','gy','gz'}, dimensions={0}, use_global_device_ids=true | all-gather | bytes 263168 | tf_op jit(solution)/shard_map/all_gather | solution.py:142
  276.2 4.3 fusion.23
  282.0 4.0 collective-permute-start.13
  307.2 76.2 %psum.44 = f32[8]{0:T(128)S(1)} all-reduce(f32[8]{0:T(128)S(1)} %multiply_reduce_fusion.3), channel_id=1, replica_groups=mesh['gx'=8,'gy'=4,'gz'=8] {'gx','gy','gz'}, use_global_device_ids=true, to_apply=%region_5.7 | all-reduce | flops 8 | bytes 64 | tf_op jit(solution)/shard_map/psum | solution.py:127
  383.5 4.3 fusion.41
  389.2 4.3 collective-permute-start.19
  400.5 5.3 collective-permute-start.23
  414.6 77.4 %psum.45 = f32[8]{0:T(128)S(1)} all-reduce(f32[8]{0:T(128)S(1)} %multiply_reduce_fusion.2), channel_id=1, replica_groups=mesh['gx'=8,'gy'=4,'gz'=8] {'gx','gy','gz'}, use_global_device_ids=true, to_apply=%region_7.9 | all-reduce | flops 8 | bytes 64 | tf_op jit(solution)/shard_map/psum | solution.py:138
  492.2 61.6 %all-gather.2 = f32[256,32,8]{1,2,0:T(8,128)S(1)} all-gather(f32[1,32,8]{1,2,0:T(8,128)S(1)} %fusion.48), channel_id=1, replica_groups=mesh['gx'=8,'gy'=4,'gz'=8] {'gx','gy','gz'}, dimensions={0}, use_global_device_ids=true | all-gather | bytes 263168 | tf_op jit(solution)/shard_map/all_gather | solution.py:142
  555.7 4.3 fusion.29
  586.6 76.2 %psum.46 = f32[8]{0:T(128)S(1)} all-reduce(f32[8]{0:T(128)S(1)} %multiply_reduce_fusion.1), channel_id=1, replica_groups=mesh['gx'=8,'gy'=4,'gz'=8] {'gx','gy','gz'}, use_global_device_ids=true, to_apply=%region_9.11 | all-reduce | flops 8 | bytes 64 | tf_op jit(solution)/shard_map/psum | solution.py:127
  662.9 4.3 fusion.44
  668.7 4.3 collective-permute-start.31
  679.9 5.5 collective-permute-start.35
  694.3 77.4 %psum.47 = f32[8]{0:T(128)S(1)} all-reduce(f32[8]{0:T(128)S(1)} %multiply_reduce_fusion), channel_id=1, replica_groups=mesh['gx'=8,'gy'=4,'gz'=8] {'gx','gy','gz'}, use_global_device_ids=true, to_apply=%region_11.13 | all-reduce | flops 8 | bytes 64 | tf_op jit(solution)/shard_map/psum | solution.py:138
  772.5 61.6 %all-gather.3 = f32[256,32,8]{1,2,0:T(8,128)S(1)} all-gather(f32[1,32,8]{1,2,0:T(8,128)S(1)} %fusion.47), channel_id=1, replica_groups=mesh['gx'=8,'gy'=4,'gz'=8] {'gx','gy','gz'}, dimensions={0}, use_global_device_ids=true | all-gather | bytes 263168 | tf_op jit(solution)/shard_map/all_gather | solution.py:142
  835.9 4.3 fusion.35
  (356 shorter events, 163.0 us)
Async XLA Ops:
  77.6 5.4 collective-permute-start
  91.2 6.3 collective-permute-start.5
  95.3 5.0 collective-permute-start.4
  108.2 5.9 collective-permute-start.6
  109.6 5.3 collective-permute-start.7
  123.1 6.5 collective-permute-start.11
  127.6 5.0 collective-permute-start.10
  280.6 5.4 collective-permute-start.12
  294.5 6.3 collective-permute-start.17
  298.6 5.0 collective-permute-start.16
  387.9 5.7 collective-permute-start.18
  389.2 5.1 collective-permute-start.19
  400.5 7.8 collective-permute-start.23
  406.0 5.0 collective-permute-start.22
  560.1 5.4 collective-permute-start.24
  574.0 6.3 collective-permute-start.29
  578.0 5.0 collective-permute-start.28
  667.3 5.7 collective-permute-start.30
  668.7 5.1 collective-permute-start.31
  679.9 7.8 collective-permute-start.35
  685.6 5.0 collective-permute-start.34
  840.4 5.4 collective-permute-start.36
  854.2 6.3 collective-permute-start.41
  858.3 5.0 collective-permute-start.40
  (22 other events, 305.5 us)
where the time goes:
time: 878 us; the launch traced here: 868 us
  blocking collectives  636 us (72%)
  starting transfers between devices  109 us (12%)
  waiting for transfers between devices  42.2 us (5%)
  local copies, waits for them, and re-layouts  37.7 us (4%)
  matrix products  36 us (4%)
    all_gather x4, blocking collectives, body(): lax.all_gather(coefficients(residual), ('gx', 'gy', 'gz'), axis=1, tiled=...  252 us
    psum x3, blocking collectives, global_inner(): lax.psum(jnp.sum(weight * former * latter, axis=1), ('gx', 'gy', 'gz'))  229 us
    psum x2, blocking collectives, body(): curvature = lax.psum(partial_curve, ('gx', 'gy', 'gz'))  155 us
    ppermute x42, starting transfers between devices, from_behind(): return lax.ppermute(block, axis, route)  109 us
    ppermute x42, waiting for transfers between devices, from_behind(): return lax.ppermute(block, axis, route)  42.2 us
    dot_general x11, matrix products, product(): jnp.dot(former, latter, precision=lax.Precision.HIGHEST, preferred_elemen...  30.7 us
    gather x14, local copies, waits for them, and re-layouts, assemble(): return values + paired * jnp.take(arrived, partner, axis=1)  20.8 us
  transfers between devices with their start and end apart: 42, of which 21 were waited for; matrix products, arithmetic and copies ran while one was open for 1% of the time, Pallas kernels for 0%

commit v1 on v0

v1 whole, which is shorter than its diff:
```python
import functools

import jax
import jax.numpy as jnp
from jax import lax
from jax.experimental import pallas as pl
from jax.experimental.pallas import tpu as pltpu
from jax.sharding import PartitionSpec as P

FACE_SLOTS = 144
EDGE_SLOTS = 12
CORNER_SLOTS = 2
DUAL_STEPS = 3
LANES = 128
MESH = pl.DeviceIdType.MESH


def block_list():
    blocks = []
    cursor = 0
    for first in (-1, 0, 1):
        for second in (-1, 0, 1):
            for third in (-1, 0, 1):
                nonzero = abs(first) + abs(second) + abs(third)
                if nonzero == 0:
                    continue
                extent = (FACE_SLOTS, EDGE_SLOTS, CORNER_SLOTS)[nonzero - 1]
                blocks.append(((first, second, third), cursor, extent))
                cursor += extent
    return blocks


BLOCKS = block_list()
SPAN = {d: (start, start + extent) for d, start, extent in BLOCKS}


def opposite(d):
    return (-d[0], -d[1], -d[2])


def tiles_of(d):
    start, stop = SPAN[d]
    return start // LANES, (stop - 1) // LANES + 1


def arrival_places():
    places = {}
    cursor = 0
    for d, _, _ in BLOCKS:
        first, last = tiles_of(opposite(d))
        places[d] = cursor
        cursor += last - first
    return places, cursor


PLACES, ARRIVING = arrival_places()


def merge_plan(tile):
    plan = []
    for d, _, _ in sorted(BLOCKS, key=lambda record: SPAN[opposite(record[0])]):
        source = opposite(d)
        first, last = tiles_of(source)
        if first <= tile < last:
            plan.append((min(SPAN[source][1] - tile * LANES, LANES), PLACES[d] + tile - first))
    return plan


def sources_of(tile):
    found = set()
    for d, _, _ in BLOCKS:
        first, last = tiles_of(d)
        if first <= tile < last:
            found.update(range(*tiles_of(opposite(d))))
    return sorted(found)


def in_parts(values):
    leading = values.astype(jnp.bfloat16).astype(jnp.float32)
    return jnp.concatenate([values, values - leading], axis=0).astype(jnp.bfloat16)


def fold_rows(values):
    rows = values.shape[0] // 2
    return values[:rows] + values[rows:]


def product(rows, table):
    parts = in_parts(rows)
    whole = jnp.dot(parts, table[1], preferred_element_type=jnp.float32)
    whole += jnp.dot(parts, table[0], preferred_element_type=jnp.float32)
    return fold_rows(whole)


def contract_last(rows, table):
    whole = lax.dot_general(
        in_parts(rows), table, (((1,), (1,)), ((), ())), preferred_element_type=jnp.float32
    )
    whole = fold_rows(whole)
    half = whole.shape[1] // 2
    return whole[:, :half] + whole[:, half:]


def kernel(
    sizes,
    rhs_hbm,
    dual_hbm,
    dirichlet_hbm,
    modes_hbm,
    coarse_hbm,
    partner_hbm,
    sign_hbm,
    count_ref,
    x_ref,
    z_ref,
    modes,
    partner,
    sign_int,
    stage_dual,
    stage_dirichlet,
    dual,
    dirichlet,
    coarse_line,
    coarse_table,
    modes_send,
    modes_field,
    line_third,
    line_first,
    line_second,
    outgoing,
    arriving,
    residual,
    direction,
    mapped,
    local_residual,
    local_mapped,
    small,
    sign_ref,
    weight_ref,
    lane_ref,
    tile_ref,
    local_sem,
    rows_sem,
    line_send,
    line_recv,
    halo_send,
    halo_recv,
):
    place = (lax.axis_index("gx"), lax.axis_index("gy"), lax.axis_index("gz"))
    loads, order = rhs_hbm.shape
    modes_total = modes_hbm.shape[0]
    span_columns = coarse_line.shape[1] // sizes[0]

    def shifted(shifts):
        return tuple(
            lax.rem(place[i] + shifts[i] + sizes[i], sizes[i]) if shifts[i] else place[i]
            for i in range(3)
        )

    def along(axis, distance):
        shifts = [0, 0, 0]
        shifts[axis] = distance
        return shifted(shifts)

    loading = [
        pltpu.make_async_copy(rhs_hbm, residual, local_sem.at[0]),
        pltpu.make_async_copy(modes_hbm, modes, local_sem.at[1]),
        pltpu.make_async_copy(sign_hbm, sign_int, local_sem.at[2]),
        pltpu.make_async_copy(partner_hbm, partner, local_sem.at[3]),
        pltpu.make_async_copy(dirichlet_hbm, stage_dirichlet, local_sem.at[4]),
        pltpu.make_async_copy(dual_hbm, stage_dual, local_sem.at[5]),
    ]
    for copy in loading:
        copy.start()

    partners = [d for d, _, _ in BLOCKS]
    for axis in range(3):
        for distance in range(2, sizes[axis] - 1):
            shifts = [0, 0, 0]
            shifts[axis] = distance
            partners.append(tuple(shifts))
    barrier = pltpu.get_barrier_semaphore()
    for shifts in partners:
        pl.semaphore_signal(barrier, inc=1, device_id=shifted(shifts), device_id_type=MESH)

    slot = lax.broadcasted_iota(jnp.int32, (loads, order), 1)
    paired = jnp.zeros((loads, order), jnp.int32)
    for d, start, extent in BLOCKS:
        inside = jnp.int32(1)
        for axis in range(3):
            if d[axis] == -1:
                inside = inside * jnp.where(place[axis] > 0, 1, 0)
            if d[axis] == 1:
                inside = inside * jnp.where(place[axis] < sizes[axis] - 1, 1, 0)
        paired = jnp.where((slot >= start) & (slot < start + extent), inside, paired)
    weight_ref[...] = 1.0 - 0.5 * paired.astype(jnp.float32)
    loading[2].wait()
    sign_ref[...] = jnp.broadcast_to(sign_int[...], (loads, order)).astype(jnp.float32)
    loading[3].wait()
    spread = jnp.broadcast_to(partner[...], (loads, order))
    lane_ref[...] = spread & (LANES - 1)
    tile_ref[...] = jnp.where(paired > 0, spread >> 7, -1)

    loading[1].wait()
    row = lax.broadcasted_iota(jnp.int32, (modes_total, order), 0)
    used = jnp.where(row < count_ref[0], modes[...], 0.0)
    leading = used.astype(jnp.bfloat16)
    remaining = (used - leading.astype(jnp.float32)).astype(jnp.bfloat16)
    modes_send[...] = jnp.zeros_like(modes_send)
    modes_field[...] = jnp.zeros_like(modes_field)
    quarter = pl.multiple_of(lax.rem(place[2], 4) * modes_total, modes_total)
    modes_send[pl.ds(quarter, modes_total), :] = leading
    modes_send[pl.ds(LANES + quarter, modes_total), :] = remaining
    own_rows = pl.ds(pl.multiple_of(place[1] * modes_total, modes_total), modes_total)
    modes_field[0, own_rows, :] = leading
    modes_field[1, own_rows, :] = remaining

    loading[0].wait()
    pl.semaphore_wait(barrier, len(partners))

    def line_start(axis, buffer, stage, message):
        buffer[stage, place[axis]] = message
        for distance in range(1, sizes[axis]):
            pltpu.make_async_remote_copy(
                src_ref=buffer.at[stage, place[axis]],
                dst_ref=buffer.at[stage, place[axis]],
                send_sem=line_send.at[stage, axis],
                recv_sem=line_recv.at[stage, axis],
                device_id=along(axis, distance),
                device_id_type=MESH,
            ).start()

    def line_wait(axis, buffer, stage):
        others = buffer.at[stage, pl.ds(0, sizes[axis] - 1)]
        copy = pltpu.make_async_remote_copy(
            src_ref=others,
            dst_ref=others,
            send_sem=line_send.at[stage, axis],
            recv_sem=line_recv.at[stage, axis],
            device_id=along(axis, 1),
            device_id_type=MESH,
        )
        copy.wait_recv()
        copy.wait_send()

    def gather_start(stage, values, sums):
        message = jnp.concatenate([contract_last(values, modes_send[...]), sums], axis=1)
        line_start(2, line_third, stage, message)

    def gather_middle(stage):
        line_wait(2, line_third, stage)
        half = sizes[2] // 2
        groups = []
        sums = jnp.zeros((loads, LANES), jnp.float32)
        for group in range(2):
            total = jnp.zeros((loads, LANES), jnp.float32)
            for number in range(group * half, group * half + half):
                total += line_third[stage, number, :, :LANES]
                sums += line_third[stage, number, :, LANES:]
            groups.append(total)
        line_start(0, line_first, stage, jnp.concatenate(groups + [sums], axis=1))

    def gather_last(stage):
        line_wait(0, line_first, stage)
        pieces = []
        sums = jnp.zeros((loads, LANES), jnp.float32)
        for number in range(sizes[0]):
            pieces.append(line_first[stage, number, :, :span_columns])
            sums += line_first[stage, number, :, span_columns:]
        partial = contract_last(jnp.concatenate(pieces, axis=1), coarse_table[...])
        line_start(1, line_second, stage, jnp.concatenate([partial, sums], axis=1))

    def gather_end(stage):
        line_wait(1, line_second, stage)
        total = line_second[stage, 0]
        for number in range(1, sizes[1]):
            total += line_second[stage, number]
        return total[:, :LANES], total[:, LANES:]

    def halo_start(phase, values):
        outgoing[phase] = values
        for d, _, _ in BLOCKS:
            first, last = tiles_of(d)
            at = PLACES[opposite(d)]
            pltpu.make_async_remote_copy(
                src_ref=outgoing.at[phase, :, pl.ds(first * LANES, (last - first) * LANES)],
                dst_ref=arriving.at[phase, :, pl.ds(at * LANES, (last - first) * LANES)],
                send_sem=halo_send.at[phase],
                recv_sem=halo_recv.at[phase],
                device_id=shifted(d),
                device_id_type=MESH,
            ).start()

    def halo_end(phase):
        copy = pltpu.make_async_remote_copy(
            src_ref=arriving.at[phase],
            dst_ref=arriving.at[phase],
            send_sem=halo_send.at[phase],
            recv_sem=halo_recv.at[phase],
            device_id=shifted(BLOCKS[0][0]),
            device_id_type=MESH,
        )
        copy.wait_recv()
        copy.wait_send()
        lane = lax.broadcasted_iota(jnp.int32, (loads, LANES), 1)
        tiles = []
        for tile in range(order // LANES):
            plan = merge_plan(tile)
            merged = None
            for stop, at in reversed(plan):
                piece = arriving[phase, :, at * LANES : (at + 1) * LANES]
                merged = piece if merged is None else jnp.where(lane < stop, piece, merged)
            tiles.append(merged)
        results = []
        for tile in range(order // LANES):
            here = slice(tile * LANES, (tile + 1) * LANES)
            taken = jnp.zeros((loads, LANES), jnp.float32)
            for source in sources_of(tile):
                moved = jnp.take_along_axis(
                    tiles[source], lane_ref[:, here], axis=1, mode="promise_in_bounds"
                )
                taken = jnp.where(tile_ref[:, here] == source, moved, taken)
            results.append(outgoing[phase, :, here] + taken)
        return jnp.concatenate(results, axis=1)

    def local_term(values):
        scaled = weight_ref[...] * sign_ref[...]
        return scaled * product(scaled * values, dirichlet)

    def split_table(source, table):
        step = 64

        def body(i, carry):
            rows = pl.ds(pl.multiple_of(i * step, step), step)
            values = source[rows, :]
            leading = values.astype(jnp.bfloat16)
            table[0, rows, :] = leading
            table[1, rows, :] = (values - leading.astype(jnp.float32)).astype(jnp.bfloat16)
            return carry

        lax.fori_loop(0, order // step, body, 0)

    def inner(former, latter):
        whole = weight_ref[...] * former * latter
        total = whole[:, :LANES]
        for tile in range(1, order // LANES):
            total += whole[:, tile * LANES : (tile + 1) * LANES]
        return jnp.sum(total, axis=1, keepdims=True)

    def in_lanes(columns):
        lane = lax.broadcasted_iota(jnp.int32, (loads, LANES), 1)
        tile = jnp.zeros((loads, LANES), jnp.float32)
        for number, column in enumerate(columns):
            tile = jnp.where(lane == number, column, tile)
        return tile

    gather_start(0, residual[...], jnp.zeros((loads, LANES), jnp.float32))

    def rows_copy(first, target, peer):
        source = coarse_hbm.at[
            :, pl.ds(pl.multiple_of((first * sizes[1] + target) * span_columns, span_columns), span_columns)
        ]
        goal = coarse_line.at[
            pl.ds(pl.multiple_of(place[1] * modes_total, modes_total), modes_total),
            pl.ds(pl.multiple_of(first * span_columns, span_columns), span_columns),
        ]
        if peer is None:
            return pltpu.make_async_copy(source, goal, local_sem.at[6])
        return pltpu.make_async_remote_copy(
            src_ref=source,
            dst_ref=goal,
            send_sem=rows_sem.at[0],
            recv_sem=rows_sem.at[1],
            device_id=peer,
            device_id_type=MESH,
        )

    for distance in range(1, sizes[1]):
        peer = along(1, distance)

        def send_rows(first, carry, peer=peer):
            rows_copy(first, peer[1], peer).start()
            return carry

        lax.fori_loop(0, sizes[0], send_rows, 0)

    def keep_rows(first, carry):
        rows_copy(first, place[1], None).start()
        return carry

    lax.fori_loop(0, sizes[0], keep_rows, 0)

    loading[4].wait()
    split_table(stage_dirichlet, dirichlet)
    gather_middle(0)
    local_residual[...] = local_term(residual[...])
    loading[5].wait()
    split_table(stage_dual, dual)

    others = coarse_line.at[pl.ds(0, (sizes[1] - 1) * modes_total), :]
    rows_wait = pltpu.make_async_remote_copy(
        src_ref=others,
        dst_ref=others,
        send_sem=rows_sem.at[0],
        recv_sem=rows_sem.at[1],
        device_id=along(1, 1),
        device_id_type=MESH,
    )
    rows_wait.wait_recv()
    rows_wait.wait_send()
    own = coarse_line.at[pl.ds(0, modes_total), :]
    pltpu.make_async_copy(own, own, local_sem.at[6]).wait()
    rows = coarse_line[...]
    leading = rows.astype(jnp.bfloat16)
    coarse_table[:LANES, :] = leading
    coarse_table[LANES:, :] = (rows - leading.astype(jnp.float32)).astype(jnp.bfloat16)

    gather_last(0)
    zeros = jnp.zeros((loads, order), jnp.float32)
    direction[...] = zeros
    mapped[...] = zeros
    local_mapped[...] = zeros
    x_ref[...] = zeros
    coarse, _ = gather_end(0)
    small[0] = coarse
    small[1] = jnp.zeros((loads, LANES), jnp.float32)
    small[2] = jnp.ones((loads, LANES), jnp.float32)
    halo_start(0, local_residual[...] + product(coarse, modes_field))
    z_ref[...] = halo_end(0)

    def step(number, carry):
        stage = number + 1
        image = 2 * number + 1
        sign = sign_ref[...]
        conditioned = z_ref[...]
        halo_start(image, sign * product(sign * conditioned, dual))
        energy_part = inner(residual[...], conditioned)
        cross_part = inner(conditioned, mapped[...])
        fresh = halo_end(image)
        curve_part = inner(conditioned, fresh)
        other_part = inner(direction[...], fresh)
        gather_start(stage, fresh, in_lanes([energy_part, cross_part, curve_part, other_part]))
        fresh_local = local_term(fresh)
        gather_middle(stage)
        gather_last(stage)
        fresh_coarse, sums = gather_end(stage)

        energy = sums[:, 0:1]
        energy_before = small[2, :, 0:1]
        curve_before = small[2, :, 1:2]
        beta = jnp.where(number == 0, 0.0, energy / energy_before)
        curve = sums[:, 2:3] + beta * (sums[:, 1:2] + sums[:, 3:4]) + beta * beta * curve_before
        alpha = energy / curve
        small[2] = in_lanes([energy, curve])

        coarse_mapped = fresh_coarse + beta * small[1]
        coarse_residual = small[0] - alpha * coarse_mapped
        small[1] = coarse_mapped
        small[0] = coarse_residual
        local_image = fresh_local + beta * local_mapped[...]
        local_mapped[...] = local_image
        local_now = local_residual[...] - alpha * local_image
        local_residual[...] = local_now
        halo_start(image + 1, local_now + product(coarse_residual, modes_field))

        along_now = conditioned + beta * direction[...]
        direction[...] = along_now
        mapped_now = fresh + beta * mapped[...]
        mapped[...] = mapped_now
        x_ref[...] = x_ref[...] + alpha * along_now
        residual[...] = residual[...] - alpha * mapped_now
        z_ref[...] = halo_end(image + 1)
        return carry

    lax.fori_loop(0, DUAL_STEPS, step, 0)


def body(
    sizes,
    adjoint_rhs,
    dual_operator,
    dirichlet,
    geneo_modes,
    coarse_inverse,
    partner_slot,
    jump_sign,
    mode_count,
):
    loads, order = adjoint_rhs.shape[3:]
    modes_total, coarse_size = coarse_inverse.shape[3:]
    columns = coarse_size // sizes[1]
    stages = DUAL_STEPS + 1
    phases = 2 * DUAL_STEPS + 1
    vector = pltpu.VMEM((loads, order), jnp.float32)
    whole = jax.ShapeDtypeStruct((loads, order), jnp.float32)

    def run(*args):

        return pl.pallas_call(
            functools.partial(kernel, sizes),
            out_shape=(whole, whole),
            in_specs=[pl.BlockSpec(memory_space=pl.ANY)] * 7
            + [pl.BlockSpec(memory_space=pltpu.SMEM)],
            out_specs=(
                pl.BlockSpec(memory_space=pltpu.VMEM),
                pl.BlockSpec(memory_space=pltpu.VMEM),
            ),
            scratch_shapes=[
                pltpu.VMEM((modes_total, order), jnp.float32),
                pltpu.VMEM((1, order), jnp.int32),
                pltpu.VMEM((1, order), jnp.int32),
                pltpu.VMEM((order, order), jnp.float32),
                pltpu.VMEM((order, order), jnp.float32),
                pltpu.VMEM((2, order, order), jnp.bfloat16),
                pltpu.VMEM((2, order, order), jnp.bfloat16),
                pltpu.VMEM((LANES, columns), jnp.float32),
                pltpu.VMEM((2 * LANES, columns), jnp.bfloat16),
                pltpu.VMEM((2 * LANES, order), jnp.bfloat16),
                pltpu.VMEM((2, LANES, order), jnp.bfloat16),
                pltpu.VMEM((stages, sizes[2], loads, 2 * LANES), jnp.float32),
                pltpu.VMEM((stages, sizes[0], loads, 3 * LANES), jnp.float32),
                pltpu.VMEM((stages, sizes[1], loads, 2 * LANES), jnp.float32),
                pltpu.VMEM((phases, loads, order), jnp.float32),
                pltpu.VMEM((phases, loads, ARRIVING * LANES), jnp.float32),
                vector,
                vector,
                vector,
                vector,
                vector,
                pltpu.VMEM((3, loads, LANES), jnp.float32),
                vector,
                vector,
                pltpu.VMEM((loads, order), jnp.int32),
                pltpu.VMEM((loads, order), jnp.int32),
                pltpu.SemaphoreType.DMA((7,)),
                pltpu.SemaphoreType.DMA((2,)),
                pltpu.SemaphoreType.DMA((stages, 3)),
                pltpu.SemaphoreType.DMA((stages, 3)),
                pltpu.SemaphoreType.DMA((phases,)),
                pltpu.SemaphoreType.DMA((phases,)),
            ],
            compiler_params=pltpu.CompilerParams(
                collective_id=0, has_side_effects=True, vmem_limit_bytes=56 * 1024 * 1024
            ),
        )(*args)

    found, force = run(
        adjoint_rhs.reshape(loads, order),
        dual_operator.reshape(order, order),
        dirichlet.reshape(order, order),
        geneo_modes.reshape(modes_total, order),
        coarse_inverse.reshape(modes_total, coarse_size),
        partner_slot.reshape(1, order),
        jump_sign.reshape(1, order),
        mode_count.reshape(1),
    )
    return found.reshape(adjoint_rhs.shape), force.reshape(adjoint_rhs.shape)


def solution(mesh):

    sizes = (mesh.shape["gx"], mesh.shape["gy"], mesh.shape["gz"])
    spot = ("gx", "gy", "gz")
    placed = (
        P(*spot, None, None),
        P(*spot, None, None),
        P(*spot, None, None),
        P(*spot, None, None),
        P(*spot, None, None),
        P(*spot, None),
        P(*spot, None),
        P(*spot),
    )
    return jax.shard_map(
        functools.partial(body, sizes),
        mesh=mesh,
        in_specs=placed,
        out_specs=(P(*spot, None, None), P(*spot, None, None)),
        check_vma=False,
    )
```

time: 878 us -> 112 us (0.13); the launches traced: 868 us -> 112 us
  blocking collectives: 636 us -> 0 us
  starting transfers between devices: 109 us -> 0 us
  Pallas kernels: 0 us -> 108 us
  waiting for transfers between devices: 42.2 us -> 0 us
  matrix products: 36 us -> 0 us
  local copies, waits for them, and re-layouts: 37.7 us -> 2.75 us
    psum x5 -> x0, blocking collectives: 384 us -> none  [the longest x3 229 us: global_inner(): lax.psum(jnp.sum(weight * former * latter, axis=1), ('gx', 'gy', 'gz'))]
    all_gather x4 -> x0, blocking collectives: 252 us -> none  [body(): lax.all_gather(coefficients(residual), ('gx', 'gy', 'gz'), axis=1, tiled=...]
    ppermute x42 -> x0, starting transfers between devices: 109 us -> none  [from_behind(): return lax.ppermute(block, axis, route)]
    pallas_call x0 -> x1, Pallas kernels: none -> 108 us  [run(): pl.pallas_call(functools.partial(kernel, sizes), out_shape=(whole, whole)...]
    ppermute x42 -> x0, waiting for transfers between devices: 42.2 us -> none  [from_behind(): return lax.ppermute(block, axis, route)]
    dot_general x19 -> x0, matrix products: 36 us -> none  [the longest x11 30.7 us: product(): jnp.dot(former, latter, precision=lax.Precision.HIGHEST, preferred_elemen...]
    gather x14 -> x0, local copies, waits for them, and re-layouts: 20.8 us -> none  [assemble(): return values + paired * jnp.take(arrived, partner, axis=1)]
    slice x147 -> x0, local copies, waits for them, and re-layouts: 10.6 us -> none  [the longest x126 9.1 us: neighbour_values(): pieces[record[0]] = arrived[:, cursor:cursor + record[2]]]
  transfers between devices with their start and end apart: 42 -> 0, of which waited for: 21 -> 0; matrix products, arithmetic and copies ran while one was open for 1% -> 0% of each run, Pallas kernels for 0% -> 0%
where the time goes in v1:
time: 112 us
  Pallas kernels  108 us (96%)
  local copies, waits for them, and re-layouts  2.75 us (2%)
  between operations  1.29 us (1%)
    pallas_call x1, Pallas kernels, run(): pl.pallas_call(functools.partial(kernel, sizes), out_shape=(whole, whole)...  108 us
    unnamed x2, local copies, waits for them, and re-layouts  2.75 us

profile of v1, /device:TPU:1, one launch (start us, length us, event | category | flops | bytes accessed | tf_op | source)
XLA Modules:
  0.0 112.2 jit_solution(14080902157054555780)
XLA Ops:
  1.3 108.2 %shard_map.95 = (f32[8,1024]{1,0:T(8,128)}, f32[8,1024]{1,0:T(8,128)}) custom-call(f32[8,1024]{1,0:T(8,128)} %bitcast.15, f32[1024,1024]{1,0:T(8,128)} %bitcast.11, f32[1024,1024]{1,0:T(8,128)} %bitcast.12, f32[32,1024]{1,0:T(8,128)} %bitcast.14, f32[32,8192]{1,0:T(8,128)} %bitcast.13, s32[1,1024]{1,0:T(1,128)} %bitcast.18, s32[1,1024]{1,0:T(1,128)} %bitcast.19, ...), custom_call_target="tpu_custom_call" | custom-call | tf_op jit(solution)/shard_map/pallas_call | solution.py:499
  109.4 1.4 %copy.13 = f32[1,1,1,8,1024]{4,3,2,1,0:T(8,128)} copy(f32[1,1,1,8,1024]{4,3,2,1,0:T(8,128)} %bitcast.17) | data formatting | bytes 65536
  110.8 1.4 %copy.14 = f32[1,1,1,8,1024]{4,3,2,1,0:T(8,128)} copy(f32[1,1,1,8,1024]{4,3,2,1,0:T(8,128)} %bitcast.16) | data formatting | bytes 65536

commit v2 on v1

--- a/solution.py
+++ b/solution.py
@@ -31,6 +31,7 @@
 
 
 BLOCKS = block_list()
+FAR_FIRST = sorted((record[0] for record in BLOCKS), key=lambda d: -sum(map(abs, d)))
 SPAN = {d: (start, start + extent) for d, start, extent in BLOCKS}
 
 
@@ -110,12 +111,12 @@
     coarse_hbm,
     partner_hbm,
     sign_hbm,
-    count_ref,
-    x_ref,
-    z_ref,
+    count_hbm,
+    both,
     modes,
     partner,
     sign_int,
+    count,
     stage_dual,
     stage_dirichlet,
     dual,
@@ -124,9 +125,10 @@
     coarse_table,
     modes_send,
     modes_field,
-    line_third,
-    line_first,
-    line_second,
+    given,
+    taken_in,
+    shared,
+    shared_in,
     outgoing,
     arriving,
     residual,
@@ -140,16 +142,24 @@
     lane_ref,
     tile_ref,
     local_sem,
-    rows_sem,
-    line_send,
-    line_recv,
+    rows_send,
+    rows_recv,
+    take_send,
+    take_recv,
+    share_send,
+    share_recv,
     halo_send,
     halo_recv,
 ):
     place = (lax.axis_index("gx"), lax.axis_index("gy"), lax.axis_index("gz"))
     loads, order = rhs_hbm.shape
+    x_ref, z_ref = both.at[0], both.at[1]
     modes_total = modes_hbm.shape[0]
-    span_columns = coarse_line.shape[1] // sizes[0]
+    half = sizes[2] // 2
+    core = lax.rem(place[2], 2)
+    chip = place[2] // 2
+    side = place[2] // half
+    pack = LANES // modes_total
 
     def shifted(shifts):
         return tuple(
@@ -157,10 +167,31 @@
             for i in range(3)
         )
 
-    def along(axis, distance):
-        shifts = [0, 0, 0]
-        shifts[axis] = distance
-        return shifted(shifts)
+    def ring(distance, size):
+        return min(distance, size - distance)
+
+    takers = sorted(
+        ((first, hop) for first in range(sizes[0]) for hop in range(half)),
+        key=lambda pair: -ring(pair[0], sizes[0]) - ring(pair[1], half),
+    )[:-1]
+    sharers = sorted(
+        ((second, other) for second in range(sizes[1]) for other in range(2)),
+        key=lambda pair: -2 * ring(pair[0], sizes[1]) - pair[1],
+    )[:-1]
+
+    def taker(first, hop):
+        return (
+            lax.rem(place[0] + first, sizes[0]),
+            place[1],
+            2 * lax.rem(chip + hop, half) + side,
+        )
+
+    def sharer(second, other):
+        third = 2 * chip + (1 - core) if other else place[2]
+        return (place[0], lax.rem(place[1] + second, sizes[1]), third)
+
+    sibling = sharer(0, 1)
+    keeps = core == side
 
     loading = [
         pltpu.make_async_copy(rhs_hbm, residual, local_sem.at[0]),
@@ -169,19 +200,34 @@
         pltpu.make_async_copy(partner_hbm, partner, local_sem.at[3]),
         pltpu.make_async_copy(dirichlet_hbm, stage_dirichlet, local_sem.at[4]),
         pltpu.make_async_copy(dual_hbm, stage_dual, local_sem.at[5]),
+        pltpu.make_async_copy(count_hbm, count, local_sem.at[7]),
     ]
     for copy in loading:
         copy.start()
 
-    partners = [d for d, _, _ in BLOCKS]
-    for axis in range(3):
-        for distance in range(2, sizes[axis] - 1):
-            shifts = [0, 0, 0]
-            shifts[axis] = distance
-            partners.append(tuple(shifts))
     barrier = pltpu.get_barrier_semaphore()
-    for shifts in partners:
-        pl.semaphore_signal(barrier, inc=1, device_id=shifted(shifts), device_id_type=MESH)
+    greeted = 0
+    for d in FAR_FIRST:
+        pl.semaphore_signal(barrier, inc=1, device_id=shifted(d), device_id_type=MESH)
+        greeted += 1
+    def greet_giver(first, hop):
+        third = half * core + lax.rem(place[2] + hop, half)
+        giver = (lax.rem(place[0] + first, sizes[0]), place[1], third)
+        pl.semaphore_signal(barrier, inc=1, device_id=giver, device_id_type=MESH)
+
+    for first, hop in takers:
+        greet_giver(first, hop)
+        greeted += 1
+
+    @pl.when(jnp.logical_not(keeps))
+    def _():
+        greet_giver(0, 0)
+
+    for second, other in sharers:
+        pl.semaphore_signal(
+            barrier, inc=1, device_id=sharer(second, other), device_id_type=MESH
+        )
+        greeted += 1
 
     slot = lax.broadcasted_iota(jnp.int32, (loads, order), 1)
     paired = jnp.zeros((loads, order), jnp.int32)
@@ -202,13 +248,15 @@
     tile_ref[...] = jnp.where(paired > 0, spread >> 7, -1)
 
     loading[1].wait()
+    loading[6].wait()
     row = lax.broadcasted_iota(jnp.int32, (modes_total, order), 0)
-    used = jnp.where(row < count_ref[0], modes[...], 0.0)
+    used = jnp.where(row < count[0, 0], modes[...], 0.0)
     leading = used.astype(jnp.bfloat16)
     remaining = (used - leading.astype(jnp.float32)).astype(jnp.bfloat16)
     modes_send[...] = jnp.zeros_like(modes_send)
     modes_field[...] = jnp.zeros_like(modes_field)
-    quarter = pl.multiple_of(lax.rem(place[2], 4) * modes_total, modes_total)
+    spare = lax.rem(place[2] + 1, pack) * modes_total
+    quarter = pl.multiple_of(lax.rem(place[2], pack) * modes_total, modes_total)
     modes_send[pl.ds(quarter, modes_total), :] = leading
     modes_send[pl.ds(LANES + quarter, modes_total), :] = remaining
     own_rows = pl.ds(pl.multiple_of(place[1] * modes_total, modes_total), modes_total)
@@ -216,70 +264,100 @@
     modes_field[1, own_rows, :] = remaining
 
     loading[0].wait()
-    pl.semaphore_wait(barrier, len(partners))
-
-    def line_start(axis, buffer, stage, message):
-        buffer[stage, place[axis]] = message
-        for distance in range(1, sizes[axis]):
-            pltpu.make_async_remote_copy(
-                src_ref=buffer.at[stage, place[axis]],
-                dst_ref=buffer.at[stage, place[axis]],
-                send_sem=line_send.at[stage, axis],
-                recv_sem=line_recv.at[stage, axis],
-                device_id=along(axis, distance),
-                device_id_type=MESH,
-            ).start()
-
-    def line_wait(axis, buffer, stage):
-        others = buffer.at[stage, pl.ds(0, sizes[axis] - 1)]
-        copy = pltpu.make_async_remote_copy(
-            src_ref=others,
-            dst_ref=others,
-            send_sem=line_send.at[stage, axis],
-            recv_sem=line_recv.at[stage, axis],
-            device_id=along(axis, 1),
+    pl.semaphore_wait(barrier, greeted + jnp.where(keeps, 0, 1))
+
+    def remote(source, goal, sems, index, peer):
+        return pltpu.make_async_remote_copy(
+            src_ref=source,
+            dst_ref=goal,
+            send_sem=sems[0].at[index],
+            recv_sem=sems[1].at[index],
+            device_id=peer,
             device_id_type=MESH,
         )
+
+    def wait_for(buffer, sems, index):
+        copy = remote(buffer, buffer, sems, index, sibling)
         copy.wait_recv()
         copy.wait_send()
 
+    take_sems = (take_send, take_recv)
+    share_sems = (share_send, share_recv)
+
     def gather_start(stage, values, sums):
-        message = jnp.concatenate([contract_last(values, modes_send[...]), sums], axis=1)
-        line_start(2, line_third, stage, message)
+        message = contract_last(values, modes_send[...]) + in_lanes(sums, spare)
+        own = place[0] * half + lax.rem(place[2], half)
+        given[stage] = message
+
+        def give(peer):
+            remote(given.at[stage], taken_in.at[stage, own], take_sems, stage, peer).start()
+
+        for first, hop in takers:
+            give(taker(first, hop))
+
+        @pl.when(keeps)
+        def _():
+            taken_in[stage, own] = message
+
+        @pl.when(jnp.logical_not(keeps))
+        def _():
+            give(sibling)
 
     def gather_middle(stage):
-        line_wait(2, line_third, stage)
-        half = sizes[2] // 2
-        groups = []
+        count = sizes[0] * half
+
+        @pl.when(keeps)
+        def _():
+            wait_for(taken_in.at[stage, pl.ds(0, count - 1)], take_sems, stage)
+
+        @pl.when(jnp.logical_not(keeps))
+        def _():
+            wait_for(taken_in.at[stage, pl.ds(0, count)], take_sems, stage)
+
+        pieces = []
+        held = [None] * half
+        lane = lax.broadcasted_iota(jnp.int32, (loads, LANES), 1)
         sums = jnp.zeros((loads, LANES), jnp.float32)
-        for group in range(2):
-            total = jnp.zeros((loads, LANES), jnp.float32)
-            for number in range(group * half, group * half + half):
-                total += line_third[stage, number, :, :LANES]
-                sums += line_third[stage, number, :, LANES:]
-            groups.append(total)
-        line_start(0, line_first, stage, jnp.concatenate(groups + [sums], axis=1))
-
-    def gather_last(stage):
-        line_wait(0, line_first, stage)
-        pieces = []
-        sums = jnp.zeros((loads, LANES), jnp.float32)
-        for number in range(sizes[0]):
-            pieces.append(line_first[stage, number, :, :span_columns])
-            sums += line_first[stage, number, :, span_columns:]
+        for first in range(sizes[0]):
+            total = None
+            for number in range(half):
+                piece = taken_in[stage, first * half + number]
+                total = piece if number == 0 else jnp.where(lane < number * modes_total, total, piece)
+                held[number] = piece if first == 0 else held[number] + piece
+            pieces.append(total)
+        for number in range(half):
+            start = (number + 1) % pack * modes_total
+            inside = (lane >= start) & (lane < start + modes_total)
+            sums += jnp.where(inside, held[number], 0.0)
         partial = contract_last(jnp.concatenate(pieces, axis=1), coarse_table[...])
-        line_start(1, line_second, stage, jnp.concatenate([partial, sums], axis=1))
+        message = jnp.concatenate([partial[:, :LANES], sums, partial[:, LANES:], sums], axis=1)
+        shared[stage] = message
+        own = core * sizes[1] + place[1]
+        for second, other in sharers:
+            mine = (1 - core) if other else core
+            part = pl.ds(pl.multiple_of(mine * 2 * LANES, 2 * LANES), 2 * LANES)
+            remote(
+                shared.at[stage, :, part],
+                shared_in.at[stage, own],
+                share_sems,
+                stage,
+                sharer(second, other),
+            ).start()
+        shared_in[stage, own] = jnp.where(core == 0, message[:, : 2 * LANES], message[:, 2 * LANES :])
 
     def gather_end(stage):
-        line_wait(1, line_second, stage)
-        total = line_second[stage, 0]
-        for number in range(1, sizes[1]):
-            total += line_second[stage, number]
-        return total[:, :LANES], total[:, LANES:]
+        count = 2 * sizes[1]
+        wait_for(shared_in.at[stage, pl.ds(0, count - 1)], share_sems, stage)
+        total = shared_in[stage, 0]
+        for number in range(1, count):
+            total += shared_in[stage, number]
+        sums = total[:, LANES:]
+        sums = sums + pltpu.roll(sums, LANES // 2, 1)
+        return total[:, :LANES], sums + pltpu.roll(sums, LANES // 4, 1)
 
     def halo_start(phase, values):
         outgoing[phase] = values
-        for d, _, _ in BLOCKS:
+        for d in FAR_FIRST:
             first, last = tiles_of(d)
             at = PLACES[opposite(d)]
             pltpu.make_async_remote_copy(
@@ -347,75 +425,59 @@
             total += whole[:, tile * LANES : (tile + 1) * LANES]
         return jnp.sum(total, axis=1, keepdims=True)
 
-    def in_lanes(columns):
-        lane = lax.broadcasted_iota(jnp.int32, (loads, LANES), 1)
+    def in_lanes(columns, start=0):
+        lane = lax.broadcasted_iota(jnp.int32, (loads, LANES), 1) - start
         tile = jnp.zeros((loads, LANES), jnp.float32)
         for number, column in enumerate(columns):
             tile = jnp.where(lane == number, column, tile)
         return tile
 
-    gather_start(0, residual[...], jnp.zeros((loads, LANES), jnp.float32))
-
-    def rows_copy(first, target, peer):
-        source = coarse_hbm.at[
-            :, pl.ds(pl.multiple_of((first * sizes[1] + target) * span_columns, span_columns), span_columns)
-        ]
-        goal = coarse_line.at[
-            pl.ds(pl.multiple_of(place[1] * modes_total, modes_total), modes_total),
-            pl.ds(pl.multiple_of(first * span_columns, span_columns), span_columns),
-        ]
-        if peer is None:
-            return pltpu.make_async_copy(source, goal, local_sem.at[6])
-        return pltpu.make_async_remote_copy(
-            src_ref=source,
-            dst_ref=goal,
-            send_sem=rows_sem.at[0],
-            recv_sem=rows_sem.at[1],
-            device_id=peer,
-            device_id_type=MESH,
-        )
-
-    for distance in range(1, sizes[1]):
-        peer = along(1, distance)
-
-        def send_rows(first, carry, peer=peer):
-            rows_copy(first, peer[1], peer).start()
+    gather_start(0, residual[...], [])
+
+    own_place = pl.ds(
+        pl.multiple_of(core * LANES + place[1] * modes_total, modes_total), modes_total
+    )
+
+    def rows_of(first, second, end):
+        start = ((first * sizes[1] + second) * 2 + end) * LANES
+        source = coarse_hbm.at[:, pl.ds(pl.multiple_of(start, LANES), LANES)]
+        goal = coarse_line.at[own_place, pl.ds(pl.multiple_of(first * LANES, LANES), LANES)]
+        return source, goal
+
+    rows_sems = (rows_send, rows_recv)
+    for second, other in sharers:
+        peer = sharer(second, other)
+
+        def send_rows(first, carry, peer=peer, other=other):
+            source, goal = rows_of(first, peer[1], (1 - core) if other else core)
+            remote(source, goal, rows_sems, 0, peer).start()
             return carry
 
         lax.fori_loop(0, sizes[0], send_rows, 0)
 
     def keep_rows(first, carry):
-        rows_copy(first, place[1], None).start()
+        source, goal = rows_of(first, place[1], core)
+        pltpu.make_async_copy(source, goal, local_sem.at[6]).start()
         return carry
 
     lax.fori_loop(0, sizes[0], keep_rows, 0)
 
     loading[4].wait()
     split_table(stage_dirichlet, dirichlet)
-    gather_middle(0)
     local_residual[...] = local_term(residual[...])
     loading[5].wait()
     split_table(stage_dual, dual)
 
-    others = coarse_line.at[pl.ds(0, (sizes[1] - 1) * modes_total), :]
-    rows_wait = pltpu.make_async_remote_copy(
-        src_ref=others,
-        dst_ref=others,
-        send_sem=rows_sem.at[0],
-        recv_sem=rows_sem.at[1],
-        device_id=along(1, 1),
-        device_id_type=MESH,
-    )
-    rows_wait.wait_recv()
-    rows_wait.wait_send()
+    rows_total = coarse_line.shape[0]
+    wait_for(coarse_line.at[pl.ds(0, rows_total - modes_total), :], rows_sems, 0)
     own = coarse_line.at[pl.ds(0, modes_total), :]
     pltpu.make_async_copy(own, own, local_sem.at[6]).wait()
     rows = coarse_line[...]
     leading = rows.astype(jnp.bfloat16)
-    coarse_table[:LANES, :] = leading
-    coarse_table[LANES:, :] = (rows - leading.astype(jnp.float32)).astype(jnp.bfloat16)
-
-    gather_last(0)
+    coarse_table[:rows_total, :] = leading
+    coarse_table[rows_total:, :] = (rows - leading.astype(jnp.float32)).astype(jnp.bfloat16)
+
+    gather_middle(0)
     zeros = jnp.zeros((loads, order), jnp.float32)
     direction[...] = zeros
     mapped[...] = zeros
@@ -439,10 +501,9 @@
         fresh = halo_end(image)
         curve_part = inner(conditioned, fresh)
         other_part = inner(direction[...], fresh)
-        gather_start(stage, fresh, in_lanes([energy_part, cross_part, curve_part, other_part]))
+        gather_start(stage, fresh, [energy_part, cross_part, curve_part, other_part])
         fresh_local = local_term(fresh)
         gather_middle(stage)
-        gather_last(stage)
         fresh_coarse, sums = gather_end(stage)
 
         energy = sums[:, 0:1]
@@ -488,7 +549,8 @@
 ):
     loads, order = adjoint_rhs.shape[3:]
     modes_total, coarse_size = coarse_inverse.shape[3:]
-    columns = coarse_size // sizes[1]
+    rows_total = 2 * sizes[1] * modes_total
+    columns = coarse_size // (2 * sizes[1])
     stages = DUAL_STEPS + 1
     phases = 2 * DUAL_STEPS + 1
     vector = pltpu.VMEM((loads, order), jnp.float32)
@@ -498,28 +560,26 @@
 
         return pl.pallas_call(
             functools.partial(kernel, sizes),
-            out_shape=(whole, whole),
-            in_specs=[pl.BlockSpec(memory_space=pl.ANY)] * 7
-            + [pl.BlockSpec(memory_space=pltpu.SMEM)],
-            out_specs=(
-                pl.BlockSpec(memory_space=pltpu.VMEM),
-                pl.BlockSpec(memory_space=pltpu.VMEM),
-            ),
+            out_shape=jax.ShapeDtypeStruct((2, loads, order), jnp.float32),
+            in_specs=[pl.BlockSpec(memory_space=pl.ANY)] * 8,
+            out_specs=pl.BlockSpec(memory_space=pltpu.VMEM),
             scratch_shapes=[
                 pltpu.VMEM((modes_total, order), jnp.float32),
                 pltpu.VMEM((1, order), jnp.int32),
                 pltpu.VMEM((1, order), jnp.int32),
+                pltpu.SMEM((1, 1), jnp.int32),
                 pltpu.VMEM((order, order), jnp.float32),
                 pltpu.VMEM((order, order), jnp.float32),
                 pltpu.VMEM((2, order, order), jnp.bfloat16),
                 pltpu.VMEM((2, order, order), jnp.bfloat16),
-                pltpu.VMEM((LANES, columns), jnp.float32),
-                pltpu.VMEM((2 * LANES, columns), jnp.bfloat16),
+                pltpu.VMEM((rows_total, columns), jnp.float32),
+                pltpu.VMEM((2 * rows_total, columns), jnp.bfloat16),
                 pltpu.VMEM((2 * LANES, order), jnp.bfloat16),
                 pltpu.VMEM((2, LANES, order), jnp.bfloat16),
-                pltpu.VMEM((stages, sizes[2], loads, 2 * LANES), jnp.float32),
-                pltpu.VMEM((stages, sizes[0], loads, 3 * LANES), jnp.float32),
-                pltpu.VMEM((stages, sizes[1], loads, 2 * LANES), jnp.float32),
+                pltpu.VMEM((stages, loads, LANES), jnp.float32),
+                pltpu.VMEM((stages, sizes[0] * sizes[2] // 2, loads, LANES), jnp.float32),
+                pltpu.VMEM((stages, loads, 4 * LANES), jnp.float32),
+                pltpu.VMEM((stages, 2 * sizes[1], loads, 2 * LANES), jnp.float32),
                 pltpu.VMEM((phases, loads, order), jnp.float32),
                 pltpu.VMEM((phases, loads, ARRIVING * LANES), jnp.float32),
                 vector,
@@ -532,10 +592,13 @@
                 vector,
                 pltpu.VMEM((loads, order), jnp.int32),
                 pltpu.VMEM((loads, order), jnp.int32),
-                pltpu.SemaphoreType.DMA((7,)),
-                pltpu.SemaphoreType.DMA((2,)),
-                pltpu.SemaphoreType.DMA((stages, 3)),
-                pltpu.SemaphoreType.DMA((stages, 3)),
+                pltpu.SemaphoreType.DMA((8,)),
+                pltpu.SemaphoreType.DMA((1,)),
+                pltpu.SemaphoreType.DMA((1,)),
+                pltpu.SemaphoreType.DMA((stages,)),
+                pltpu.SemaphoreType.DMA((stages,)),
+                pltpu.SemaphoreType.DMA((stages,)),
+                pltpu.SemaphoreType.DMA((stages,)),
                 pltpu.SemaphoreType.DMA((phases,)),
                 pltpu.SemaphoreType.DMA((phases,)),
             ],
@@ -544,7 +607,7 @@
             ),
         )(*args)
 
-    found, force = run(
+    both = run(
         adjoint_rhs.reshape(loads, order),
         dual_operator.reshape(order, order),
         dirichlet.reshape(order, order),
@@ -552,8 +615,9 @@
         coarse_inverse.reshape(modes_total, coarse_size),
         partner_slot.reshape(1, order),
         jump_sign.reshape(1, order),
-        mode_count.reshape(1),
+        mode_count.reshape(1, 1),
     )
+    found, force = both[0], both[1]
     return found.reshape(adjoint_rhs.shape), force.reshape(adjoint_rhs.shape)
 
 

time: 112 us -> 103 us (0.920)
  Pallas kernels: 108 us -> 101 us
  local copies, waits for them, and re-layouts: 2.75 us -> 1.4 us
    pallas_call x1, Pallas kernels: 108 us -> 101 us  [run(): pl.pallas_call(functools.partial(kernel, sizes), out_shape=jax.ShapeDtype...]
    unnamed x2 -> x0, local copies, waits for them, and re-layouts: 2.75 us -> none
    another operation x0 -> x1, local copies, waits for them, and re-layouts: none -> 1.4 us  [body(): return (found.reshape(adjoint_rhs.shape), force.reshape(adjoint_rhs.shape))]
where the time goes in v2:
time: 103 us
  Pallas kernels  101 us (98%)
  local copies, waits for them, and re-layouts  1.4 us (1%)
  between operations  1.29 us (1%)
    pallas_call x1, Pallas kernels, run(): pl.pallas_call(functools.partial(kernel, sizes), out_shape=jax.ShapeDtype...  101 us

profile of v2, /device:TPU:1, one launch (start us, length us, event | category | flops | bytes accessed | tf_op | source)
XLA Modules:
  0.0 103.3 jit_solution(8422664627811148200)
XLA Ops:
  1.3 100.6 %shard_map.95 = f32[2,8,1024]{2,1,0:T(8,128)} custom-call(f32[8,1024]{1,0:T(8,128)} %bitcast.17, f32[1024,1024]{1,0:T(8,128)} %bitcast.13, f32[1024,1024]{1,0:T(8,128)} %bitcast.14, f32[32,1024]{1,0:T(8,128)} %bitcast.16, f32[32,8192]{1,0:T(8,128)} %bitcast.15, s32[1,1024]{1,0:T(1,128)} %bitcast.18, s32[1,1024]{1,0:T(1,128)} %bitcast.19, ...), custom_call_target="tpu_custom_call" | custom-call | tf_op jit(solution)/shard_map/pallas_call | solution.py:561
  101.9 1.4 %slice_bitcast_fusion = (f32[1,1,1,8,1024]{4,3,2,1,0:T(8,128)}, f32[1,1,1,8,1024]{4,3,2,1,0:T(8,128)}) fusion(f32[2,8,1024]{2,1,0:T(8,128)} %shard_map.95), kind=kLoop, calls=%fused_computation | loop fusion | bytes 131072 | tf_op jit(solution)/shard_map/reshape;squeeze | solution.py:621

commit v3 on v2

--- a/solution.py
+++ b/solution.py
@@ -86,10 +86,11 @@
     return values[:rows] + values[rows:]
 
 
-def product(rows, table):
+def product(rows, table, start=0):
     parts = in_parts(rows)
-    whole = jnp.dot(parts, table[1], preferred_element_type=jnp.float32)
-    whole += jnp.dot(parts, table[0], preferred_element_type=jnp.float32)
+    here = slice(start, start + rows.shape[1])
+    whole = jnp.dot(parts, table[1, here], preferred_element_type=jnp.float32)
+    whole += jnp.dot(parts, table[0, here], preferred_element_type=jnp.float32)
     return fold_rows(whole)
 
 
@@ -121,21 +122,26 @@
     stage_dirichlet,
     dual,
     dirichlet,
+    coarse_own,
+    own_table,
     coarse_line,
     coarse_table,
     modes_send,
-    modes_field,
+    modes_own,
+    modes_in,
+    modes_near,
     given,
     taken_in,
     shared,
     shared_in,
+    whole_in,
+    near,
     outgoing,
     arriving,
     residual,
     direction,
     mapped,
-    local_residual,
-    local_mapped,
+    image_mapped,
     small,
     sign_ref,
     weight_ref,
@@ -148,6 +154,12 @@
     take_recv,
     share_send,
     share_recv,
+    near_send,
+    near_recv,
+    modes_sent,
+    modes_got,
+    whole_sent,
+    whole_got,
     halo_send,
     halo_recv,
 ):
@@ -190,6 +202,10 @@
         third = 2 * chip + (1 - core) if other else place[2]
         return (place[0], lax.rem(place[1] + second, sizes[1]), third)
 
+    def aside(first, way):
+        third = lax.rem(place[2] + way * (2 - 4 * core) + sizes[2], sizes[2])
+        return (lax.rem(place[0] + first + sizes[0], sizes[0]), place[1], third)
+
     sibling = sharer(0, 1)
     keeps = core == side
 
@@ -201,9 +217,10 @@
         pltpu.make_async_copy(dirichlet_hbm, stage_dirichlet, local_sem.at[4]),
         pltpu.make_async_copy(dual_hbm, stage_dual, local_sem.at[5]),
         pltpu.make_async_copy(count_hbm, count, local_sem.at[7]),
+        pltpu.make_async_copy(coarse_hbm, coarse_own, local_sem.at[8]),
     ]
-    for copy in loading:
-        copy.start()
+    for number in (0, 1, 2, 3, 6, 7, 4, 5):
+        loading[number].start()
 
     barrier = pltpu.get_barrier_semaphore()
     greeted = 0
@@ -223,6 +240,11 @@
     def _():
         greet_giver(0, 0)
 
+    for first in (-1, 0, 1):
+        pl.semaphore_signal(
+            barrier, inc=1, device_id=aside(first, -1), device_id_type=MESH
+        )
+        greeted += 1
     for second, other in sharers:
         pl.semaphore_signal(
             barrier, inc=1, device_id=sharer(second, other), device_id_type=MESH
@@ -251,17 +273,16 @@
     loading[6].wait()
     row = lax.broadcasted_iota(jnp.int32, (modes_total, order), 0)
     used = jnp.where(row < count[0, 0], modes[...], 0.0)
+    modes[...] = used
     leading = used.astype(jnp.bfloat16)
     remaining = (used - leading.astype(jnp.float32)).astype(jnp.bfloat16)
+    modes_own[0] = leading
+    modes_own[1] = remaining
     modes_send[...] = jnp.zeros_like(modes_send)
-    modes_field[...] = jnp.zeros_like(modes_field)
     spare = lax.rem(place[2] + 1, pack) * modes_total
     quarter = pl.multiple_of(lax.rem(place[2], pack) * modes_total, modes_total)
     modes_send[pl.ds(quarter, modes_total), :] = leading
     modes_send[pl.ds(LANES + quarter, modes_total), :] = remaining
-    own_rows = pl.ds(pl.multiple_of(place[1] * modes_total, modes_total), modes_total)
-    modes_field[0, own_rows, :] = leading
-    modes_field[1, own_rows, :] = remaining
 
     loading[0].wait()
     pl.semaphore_wait(barrier, greeted + jnp.where(keeps, 0, 1))
@@ -303,7 +324,7 @@
         def _():
             give(sibling)
 
-    def gather_middle(stage):
+    def collect(stage):
         count = sizes[0] * half
 
         @pl.when(keeps)
@@ -329,21 +350,18 @@
             start = (number + 1) % pack * modes_total
             inside = (lane >= start) & (lane < start + modes_total)
             sums += jnp.where(inside, held[number], 0.0)
-        partial = contract_last(jnp.concatenate(pieces, axis=1), coarse_table[...])
-        message = jnp.concatenate([partial[:, :LANES], sums, partial[:, LANES:], sums], axis=1)
+        return jnp.concatenate(pieces, axis=1), sums
+
+    def gather_middle(stage):
+        taken, sums = collect(stage)
+        partial = contract_last(taken, coarse_table[...])
+        message = jnp.concatenate([partial, sums], axis=1)
         shared[stage] = message
         own = core * sizes[1] + place[1]
+        shared_in[stage, own] = message
         for second, other in sharers:
-            mine = (1 - core) if other else core
-            part = pl.ds(pl.multiple_of(mine * 2 * LANES, 2 * LANES), 2 * LANES)
-            remote(
-                shared.at[stage, :, part],
-                shared_in.at[stage, own],
-                share_sems,
-                stage,
-                sharer(second, other),
-            ).start()
-        shared_in[stage, own] = jnp.where(core == 0, message[:, : 2 * LANES], message[:, 2 * LANES :])
+            peer = sharer(second, other)
+            remote(shared.at[stage], shared_in.at[stage, own], share_sems, stage, peer).start()
 
     def gather_end(stage):
         count = 2 * sizes[1]
@@ -351,9 +369,78 @@
         total = shared_in[stage, 0]
         for number in range(1, count):
             total += shared_in[stage, number]
-        sums = total[:, LANES:]
+        sums = total[:, 2 * LANES :]
         sums = sums + pltpu.roll(sums, LANES // 2, 1)
-        return total[:, :LANES], sums + pltpu.roll(sums, LANES // 4, 1)
+        return total[:, : 2 * LANES], sums + pltpu.roll(sums, LANES // 4, 1)
+
+    near_sems = (near_send, near_recv)
+
+    def near_start(stage, tiles):
+        near[stage, :, : 2 * LANES] = tiles
+        single = pl.ds(pl.multiple_of((1 - core) * LANES, LANES), LANES)
+        for first, at in ((1, 8), (-1, 7), (0, 6)):
+            goal = near.at[stage, :, pl.ds(at * LANES, LANES)]
+            remote(near.at[stage, :, single], goal, near_sems, stage, aside(first, 1)).start()
+        both_tiles = near.at[stage, :, pl.ds(0, 2 * LANES)]
+        for first, at in ((1, 4), (-1, 2)):
+            goal = near.at[stage, :, pl.ds(at * LANES, 2 * LANES)]
+            remote(both_tiles, goal, near_sems, stage, shifted((first, 0, 0))).start()
+
+    def near_end(stage):
+        wait_for(near.at[stage, :, pl.ds(2 * LANES, 7 * LANES)], near_sems, stage)
+        return near[stage, :, 2 * LANES :]
+
+    def modes_start():
+        for d in FAR_FIRST:
+            first, last = tiles_of(d)
+            at = PLACES[opposite(d)]
+            remote(
+                modes.at[:, pl.ds(first * LANES, (last - first) * LANES)],
+                modes_in.at[:, pl.ds(at * LANES, (last - first) * LANES)],
+                (modes_sent, modes_got),
+                0,
+                shifted(d),
+            ).start()
+
+    def modes_end():
+        wait_for(modes_in, (modes_sent, modes_got), 0)
+
+        def rows_at(d):
+            group = {0: 0, 1: 2, -1: 4}[d[0]]
+            outer = {0: 6, 1: 7, -1: 8}[d[0]]
+            if d[2] == 0:
+                tile = group + core
+            elif d[2] == 1:
+                tile = jnp.where(core == 0, group + 1, outer)
+            else:
+                tile = jnp.where(core == 1, group, outer)
+            second = lax.rem(place[1] + d[1] + sizes[1], sizes[1])
+            return pl.ds(pl.multiple_of(tile * LANES + second * modes_total, modes_total), modes_total)
+
+        def put(rows, lanes, values):
+            leading = values.astype(jnp.bfloat16)
+            modes_near[0, rows, lanes] = leading
+            modes_near[1, rows, lanes] = (values - leading.astype(jnp.float32)).astype(jnp.bfloat16)
+
+        put(rows_at((0, 0, 0)), slice(0, order), modes[...])
+        lane = lax.broadcasted_iota(jnp.int32, (modes_total, LANES), 1)
+        for d, start, extent in BLOCKS:
+            rows = rows_at(d)
+            source_first, source_last = tiles_of(opposite(d))
+            for tile in range(*tiles_of(d)):
+                here = slice(tile * LANES, (tile + 1) * LANES)
+                index = jnp.concatenate([lane_ref[:, here]] * (modes_total // loads), axis=0)
+                wanted = jnp.concatenate([tile_ref[:, here]] * (modes_total // loads), axis=0)
+                slots = lane + tile * LANES
+                wanted = jnp.where((slots >= start) & (slots < start + extent), wanted, -1)
+                taken = jnp.zeros((modes_total, LANES), jnp.float32)
+                for source in range(source_first, source_last):
+                    at = (PLACES[d] + source - source_first) * LANES
+                    moved = jnp.take_along_axis(
+                        modes_in[:, at : at + LANES], index, axis=1, mode="promise_in_bounds"
+                    )
+                    taken = jnp.where(wanted == source, moved, taken)
+                put(rows, here, taken)
 
     def halo_start(phase, values):
         outgoing[phase] = values
@@ -445,95 +532,117 @@
         return source, goal
 
     rows_sems = (rows_send, rows_recv)
+
+    def rows_start(begin, end):
+        def send_rows(first, carry):
+            for second, other in sharers:
+                peer = sharer(second, other)
+                source, goal = rows_of(first, peer[1], (1 - core) if other else core)
+                remote(source, goal, rows_sems, 0, peer).start()
+            source, goal = rows_of(first, place[1], core)
+            pltpu.make_async_copy(source, goal, local_sem.at[6]).start()
+            return carry
+
+        lax.fori_loop(begin, end, send_rows, 0)
+
+    def rows_end():
+        rows_total = coarse_line.shape[0]
+        wait_for(coarse_line.at[pl.ds(0, rows_total - modes_total), :], rows_sems, 0)
+        own = coarse_line.at[pl.ds(0, modes_total), :]
+        pltpu.make_async_copy(own, own, local_sem.at[6]).wait()
+        rows = coarse_line[...]
+        leading = rows.astype(jnp.bfloat16)
+        coarse_table[:rows_total, :] = leading
+        coarse_table[rows_total:, :] = (rows - leading.astype(jnp.float32)).astype(jnp.bfloat16)
+
+    rows_start(0, sizes[0] // 2)
+    modes_near[...] = jnp.zeros_like(modes_near)
+    loading[7].wait()
+    rows = coarse_own[...]
+    leading = rows.astype(jnp.bfloat16)
+    own_table[:modes_total, :] = leading
+    own_table[modes_total:, :] = (rows - leading.astype(jnp.float32)).astype(jnp.bfloat16)
+    loading[4].wait()
+    split_table(stage_dirichlet, dirichlet)
+    local_now = local_term(residual[...])
+
+    taken, _ = collect(0)
+    own = core * sizes[1] + place[1]
+    whole_in[own] = taken
     for second, other in sharers:
         peer = sharer(second, other)
-
-        def send_rows(first, carry, peer=peer, other=other):
-            source, goal = rows_of(first, peer[1], (1 - core) if other else core)
-            remote(source, goal, rows_sems, 0, peer).start()
-            return carry
-
-        lax.fori_loop(0, sizes[0], send_rows, 0)
-
-    def keep_rows(first, carry):
-        source, goal = rows_of(first, place[1], core)
-        pltpu.make_async_copy(source, goal, local_sem.at[6]).start()
-        return carry
-
-    lax.fori_loop(0, sizes[0], keep_rows, 0)
-
-    loading[4].wait()
-    split_table(stage_dirichlet, dirichlet)
-    local_residual[...] = local_term(residual[...])
+        remote(whole_in.at[own], whole_in.at[own], (whole_sent, whole_got), 0, peer).start()
     loading[5].wait()
     split_table(stage_dual, dual)
-
-    rows_total = coarse_line.shape[0]
-    wait_for(coarse_line.at[pl.ds(0, rows_total - modes_total), :], rows_sems, 0)
-    own = coarse_line.at[pl.ds(0, modes_total), :]
-    pltpu.make_async_copy(own, own, local_sem.at[6]).wait()
-    rows = coarse_line[...]
-    leading = rows.astype(jnp.bfloat16)
-    coarse_table[:rows_total, :] = leading
-    coarse_table[rows_total:, :] = (rows - leading.astype(jnp.float32)).astype(jnp.bfloat16)
-
-    gather_middle(0)
     zeros = jnp.zeros((loads, order), jnp.float32)
     direction[...] = zeros
     mapped[...] = zeros
-    local_mapped[...] = zeros
+    image_mapped[...] = zeros
     x_ref[...] = zeros
-    coarse, _ = gather_end(0)
-    small[0] = coarse
-    small[1] = jnp.zeros((loads, LANES), jnp.float32)
-    small[2] = jnp.ones((loads, LANES), jnp.float32)
-    halo_start(0, local_residual[...] + product(coarse, modes_field))
+    small[...] = jnp.ones((loads, LANES), jnp.float32)
+    wait_for(whole_in.at[pl.ds(0, 2 * sizes[1] - 1)], (whole_sent, whole_got), 0)
+    pieces = []
+    for first in range(sizes[0]):
+        for second in range(sizes[1]):
+            for end in range(2):
+                pieces.append(whole_in[end * sizes[1] + second, :, first * LANES : (first + 1) * LANES])
+    coarse = contract_last(jnp.concatenate(pieces, axis=1), own_table[...])
+    halo_start(0, local_now + product(coarse, modes_own))
+    rows_start(sizes[0] // 2, sizes[0] * 3 // 4)
     z_ref[...] = halo_end(0)
 
-    def step(number, carry):
+    def step(number, opening):
         stage = number + 1
         image = 2 * number + 1
         sign = sign_ref[...]
         conditioned = z_ref[...]
         halo_start(image, sign * product(sign * conditioned, dual))
+        if opening:
+            rows_start(sizes[0] * 3 // 4, sizes[0])
         energy_part = inner(residual[...], conditioned)
         cross_part = inner(conditioned, mapped[...])
         fresh = halo_end(image)
         curve_part = inner(conditioned, fresh)
         other_part = inner(direction[...], fresh)
         gather_start(stage, fresh, [energy_part, cross_part, curve_part, other_part])
-        fresh_local = local_term(fresh)
+        halo_start(image + 1, local_term(fresh))
+        if opening:
+            modes_start()
+            rows_end()
         gather_middle(stage)
-        fresh_coarse, sums = gather_end(stage)
+        if opening:
+            modes_end()
+        fresh_image = halo_end(image + 1)
+        tiles, sums = gather_end(stage)
+        near_start(stage, tiles)
 
         energy = sums[:, 0:1]
-        energy_before = small[2, :, 0:1]
-        curve_before = small[2, :, 1:2]
+        energy_before = small[:, 0:1]
+        curve_before = small[:, 1:2]
         beta = jnp.where(number == 0, 0.0, energy / energy_before)
         curve = sums[:, 2:3] + beta * (sums[:, 1:2] + sums[:, 3:4]) + beta * beta * curve_before
         alpha = energy / curve
-        small[2] = in_lanes([energy, curve])
-
-        coarse_mapped = fresh_coarse + beta * small[1]
-        coarse_residual = small[0] - alpha * coarse_mapped
-        small[1] = coarse_mapped
-        small[0] = coarse_residual
-        local_image = fresh_local + beta * local_mapped[...]
-        local_mapped[...] = local_image
-        local_now = local_residual[...] - alpha * local_image
-        local_residual[...] = local_now
-        halo_start(image + 1, local_now + product(coarse_residual, modes_field))
-
+        small[...] = in_lanes([energy, curve])
+
+        fresh_image = fresh_image + product(tiles, modes_near)
         along_now = conditioned + beta * direction[...]
         direction[...] = along_now
         mapped_now = fresh + beta * mapped[...]
         mapped[...] = mapped_now
         x_ref[...] = x_ref[...] + alpha * along_now
         residual[...] = residual[...] - alpha * mapped_now
-        z_ref[...] = halo_end(image + 1)
+        base = fresh_image + beta * image_mapped[...]
+        image_now = base + product(near_end(stage), modes_near, 2 * LANES)
+        image_mapped[...] = image_now
+        z_ref[...] = conditioned - alpha * image_now
+
+    step(0, True)
+
+    def later_step(number, carry):
+        step(number, False)
         return carry
 
-    lax.fori_loop(0, DUAL_STEPS, step, 0)
+    lax.fori_loop(1, DUAL_STEPS, later_step, 0)
 
 
 def body(
@@ -572,33 +681,44 @@
                 pltpu.VMEM((order, order), jnp.float32),
                 pltpu.VMEM((2, order, order), jnp.bfloat16),
                 pltpu.VMEM((2, order, order), jnp.bfloat16),
+                pltpu.VMEM((modes_total, coarse_size), jnp.float32),
+                pltpu.VMEM((2 * modes_total, coarse_size), jnp.bfloat16),
                 pltpu.VMEM((rows_total, columns), jnp.float32),
                 pltpu.VMEM((2 * rows_total, columns), jnp.bfloat16),
                 pltpu.VMEM((2 * LANES, order), jnp.bfloat16),
-                pltpu.VMEM((2, LANES, order), jnp.bfloat16),
+                pltpu.VMEM((2, modes_total, order), jnp.bfloat16),
+                pltpu.VMEM((modes_total, ARRIVING * LANES), jnp.float32),
+                pltpu.VMEM((2, 9 * LANES, order), jnp.bfloat16),
                 pltpu.VMEM((stages, loads, LANES), jnp.float32),
                 pltpu.VMEM((stages, sizes[0] * sizes[2] // 2, loads, LANES), jnp.float32),
-                pltpu.VMEM((stages, loads, 4 * LANES), jnp.float32),
-                pltpu.VMEM((stages, 2 * sizes[1], loads, 2 * LANES), jnp.float32),
+                pltpu.VMEM((stages, loads, 3 * LANES), jnp.float32),
+                pltpu.VMEM((stages, 2 * sizes[1], loads, 3 * LANES), jnp.float32),
+                pltpu.VMEM((2 * sizes[1], loads, columns), jnp.float32),
+                pltpu.VMEM((stages, loads, 9 * LANES), jnp.float32),
                 pltpu.VMEM((phases, loads, order), jnp.float32),
                 pltpu.VMEM((phases, loads, ARRIVING * LANES), jnp.float32),
                 vector,
                 vector,
                 vector,
                 vector,
-                vector,
-                pltpu.VMEM((3, loads, LANES), jnp.float32),
+                pltpu.VMEM((loads, LANES), jnp.float32),
                 vector,
                 vector,
                 pltpu.VMEM((loads, order), jnp.int32),
                 pltpu.VMEM((loads, order), jnp.int32),
-                pltpu.SemaphoreType.DMA((8,)),
+                pltpu.SemaphoreType.DMA((9,)),
                 pltpu.SemaphoreType.DMA((1,)),
                 pltpu.SemaphoreType.DMA((1,)),
                 pltpu.SemaphoreType.DMA((stages,)),
                 pltpu.SemaphoreType.DMA((stages,)),
                 pltpu.SemaphoreType.DMA((stages,)),
                 pltpu.SemaphoreType.DMA((stages,)),
+                pltpu.SemaphoreType.DMA((stages,)),
+                pltpu.SemaphoreType.DMA((stages,)),
+                pltpu.SemaphoreType.DMA((1,)),
+                pltpu.SemaphoreType.DMA((1,)),
+                pltpu.SemaphoreType.DMA((1,)),
+                pltpu.SemaphoreType.DMA((1,)),
                 pltpu.SemaphoreType.DMA((phases,)),
                 pltpu.SemaphoreType.DMA((phases,)),
             ],

time: 103 us -> 94.5 us (0.917)
  Pallas kernels: 101 us -> 91.1 us
    pallas_call x1, Pallas kernels: 101 us -> 91.1 us  [run(): pl.pallas_call(functools.partial(kernel, sizes), out_shape=jax.ShapeDtype...]
where the time goes in v3:
time: 94.5 us; the launch traced here: 93.8 us
  Pallas kernels  91.1 us (96%)
  local copies, waits for them, and re-layouts  1.4 us (1%)
  between operations  1.29 us (1%)
    pallas_call x1, Pallas kernels, run(): pl.pallas_call(functools.partial(kernel, sizes), out_shape=jax.ShapeDtype...  91.1 us

profile of v3, /device:TPU:1, one launch (start us, length us, event | category | flops | bytes accessed | tf_op | source)
XLA Modules:
  0.0 93.8 jit_solution(5063491219732390183)
XLA Ops:
  1.3 91.1 %shard_map.95 = f32[2,8,1024]{2,1,0:T(8,128)} custom-call(f32[8,1024]{1,0:T(8,128)} %bitcast.17, f32[1024,1024]{1,0:T(8,128)} %bitcast.13, f32[1024,1024]{1,0:T(8,128)} %bitcast.14, f32[32,1024]{1,0:T(8,128)} %bitcast.16, f32[32,8192]{1,0:T(8,128)} %bitcast.15, s32[1,1024]{1,0:T(1,128)} %bitcast.18, s32[1,1024]{1,0:T(1,128)} %bitcast.19, ...), custom_call_target="tpu_custom_call" | custom-call | tf_op jit(solution)/shard_map/pallas_call | solution.py:670
  92.4 1.4 %slice_bitcast_fusion = (f32[1,1,1,8,1024]{4,3,2,1,0:T(8,128)}, f32[1,1,1,8,1024]{4,3,2,1,0:T(8,128)}) fusion(f32[2,8,1024]{2,1,0:T(8,128)} %shard_map.95), kind=kLoop, calls=%fused_computation | loop fusion | bytes 131072 | tf_op jit(solution)/shard_map/reshape;squeeze | solution.py:741

commit v4 on v3

--- a/solution.py
+++ b/solution.py
@@ -224,9 +224,6 @@
 
     barrier = pltpu.get_barrier_semaphore()
     greeted = 0
-    for d in FAR_FIRST:
-        pl.semaphore_signal(barrier, inc=1, device_id=shifted(d), device_id_type=MESH)
-        greeted += 1
     def greet_giver(first, hop):
         third = half * core + lax.rem(place[2] + hop, half)
         giver = (lax.rem(place[0] + first, sizes[0]), place[1], third)
@@ -240,11 +237,6 @@
     def _():
         greet_giver(0, 0)
 
-    for first in (-1, 0, 1):
-        pl.semaphore_signal(
-            barrier, inc=1, device_id=aside(first, -1), device_id_type=MESH
-        )
-        greeted += 1
     for second, other in sharers:
         pl.semaphore_signal(
             barrier, inc=1, device_id=sharer(second, other), device_id_type=MESH
@@ -285,7 +277,6 @@
     modes_send[pl.ds(LANES + quarter, modes_total), :] = remaining
 
     loading[0].wait()
-    pl.semaphore_wait(barrier, greeted + jnp.where(keeps, 0, 1))
 
     def remote(source, goal, sems, index, peer):
         return pltpu.make_async_remote_copy(
@@ -305,10 +296,12 @@
     take_sems = (take_send, take_recv)
     share_sems = (share_send, share_recv)
 
-    def gather_start(stage, values, sums):
+    def gather_start(stage, values, sums, before=None):
         message = contract_last(values, modes_send[...]) + in_lanes(sums, spare)
         own = place[0] * half + lax.rem(place[2], half)
         given[stage] = message
+        if before is not None:
+            before()
 
         def give(peer):
             remote(given.at[stage], taken_in.at[stage, own], take_sems, stage, peer).start()
@@ -442,9 +435,11 @@
                     taken = jnp.where(wanted == source, moved, taken)
                 put(rows, here, taken)
 
-    def halo_start(phase, values):
-        outgoing[phase] = values
+    def halo_start(phase, values, begin=0):
+        outgoing[phase, :, begin : begin + values.shape[1]] = values
         for d in FAR_FIRST:
+            if SPAN[d][0] < begin or SPAN[d][1] > begin + values.shape[1]:
+                continue
             first, last = tiles_of(d)
             at = PLACES[opposite(d)]
             pltpu.make_async_remote_copy(
@@ -519,7 +514,10 @@
             tile = jnp.where(lane == number, column, tile)
         return tile
 
-    gather_start(0, residual[...], [])
+    def all_here():
+        pl.semaphore_wait(barrier, greeted + jnp.where(keeps, 0, 1))
+
+    gather_start(0, residual[...], [], all_here)
 
     own_place = pl.ds(
         pl.multiple_of(core * LANES + place[1] * modes_total, modes_total), modes_total
@@ -596,7 +594,12 @@
         image = 2 * number + 1
         sign = sign_ref[...]
         conditioned = z_ref[...]
-        halo_start(image, sign * product(sign * conditioned, dual))
+        parts = in_parts(sign * conditioned)
+        for begin in (0, order // 2):
+            columns = slice(begin, begin + order // 2)
+            mapped_part = jnp.dot(parts, dual[1, :, columns], preferred_element_type=jnp.float32)
+            mapped_part += jnp.dot(parts, dual[0, :, columns], preferred_element_type=jnp.float32)
+            halo_start(image, sign[:, columns] * fold_rows(mapped_part), begin)
         if opening:
             rows_start(sizes[0] * 3 // 4, sizes[0])
         energy_part = inner(residual[...], conditioned)

time: 94.5 us -> 94.5 us (level)
  no operation moved by 1% of the time
where the time goes in v4:
time: 94.5 us; the launch traced here: 94.1 us
  Pallas kernels  91.4 us (97%)
  local copies, waits for them, and re-layouts  1.4 us (1%)
  between operations  1.29 us (1%)
    pallas_call x1, Pallas kernels, run(): pl.pallas_call(functools.partial(kernel, sizes), out_shape=jax.ShapeDtype...  91.4 us

profile of v4, /device:TPU:1, one launch (start us, length us, event | category | flops | bytes accessed | tf_op | source)
XLA Modules:
  0.0 94.1 jit_solution(5900732521593995403)
XLA Ops:
  1.3 91.4 %shard_map.95 = f32[2,8,1024]{2,1,0:T(8,128)} custom-call(f32[8,1024]{1,0:T(8,128)} %bitcast.17, f32[1024,1024]{1,0:T(8,128)} %bitcast.13, f32[1024,1024]{1,0:T(8,128)} %bitcast.14, f32[32,1024]{1,0:T(8,128)} %bitcast.16, f32[32,8192]{1,0:T(8,128)} %bitcast.15, s32[1,1024]{1,0:T(1,128)} %bitcast.18, s32[1,1024]{1,0:T(1,128)} %bitcast.19, ...), custom_call_target="tpu_custom_call" | custom-call | tf_op jit(solution)/shard_map/pallas_call | solution.py:673
  92.7 1.4 %slice_bitcast_fusion = (f32[1,1,1,8,1024]{4,3,2,1,0:T(8,128)}, f32[1,1,1,8,1024]{4,3,2,1,0:T(8,128)}) fusion(f32[2,8,1024]{2,1,0:T(8,128)} %shard_map.95), kind=kLoop, calls=%fused_computation | loop fusion | bytes 131072 | tf_op jit(solution)/shard_map/reshape;squeeze | solution.py:744

commit v5 on v4

--- a/solution.py
+++ b/solution.py
@@ -243,24 +243,6 @@
         )
         greeted += 1
 
-    slot = lax.broadcasted_iota(jnp.int32, (loads, order), 1)
-    paired = jnp.zeros((loads, order), jnp.int32)
-    for d, start, extent in BLOCKS:
-        inside = jnp.int32(1)
-        for axis in range(3):
-            if d[axis] == -1:
-                inside = inside * jnp.where(place[axis] > 0, 1, 0)
-            if d[axis] == 1:
-                inside = inside * jnp.where(place[axis] < sizes[axis] - 1, 1, 0)
-        paired = jnp.where((slot >= start) & (slot < start + extent), inside, paired)
-    weight_ref[...] = 1.0 - 0.5 * paired.astype(jnp.float32)
-    loading[2].wait()
-    sign_ref[...] = jnp.broadcast_to(sign_int[...], (loads, order)).astype(jnp.float32)
-    loading[3].wait()
-    spread = jnp.broadcast_to(partner[...], (loads, order))
-    lane_ref[...] = spread & (LANES - 1)
-    tile_ref[...] = jnp.where(paired > 0, spread >> 7, -1)
-
     loading[1].wait()
     loading[6].wait()
     row = lax.broadcasted_iota(jnp.int32, (modes_total, order), 0)
@@ -435,11 +417,9 @@
                     taken = jnp.where(wanted == source, moved, taken)
                 put(rows, here, taken)
 
-    def halo_start(phase, values, begin=0):
-        outgoing[phase, :, begin : begin + values.shape[1]] = values
+    def halo_start(phase, values):
+        outgoing[phase] = values
         for d in FAR_FIRST:
-            if SPAN[d][0] < begin or SPAN[d][1] > begin + values.shape[1]:
-                continue
             first, last = tiles_of(d)
             at = PLACES[opposite(d)]
             pltpu.make_async_remote_copy(
@@ -519,6 +499,24 @@
 
     gather_start(0, residual[...], [], all_here)
 
+    slot = lax.broadcasted_iota(jnp.int32, (loads, order), 1)
+    paired = jnp.zeros((loads, order), jnp.int32)
+    for d, start, extent in BLOCKS:
+        inside = jnp.int32(1)
+        for axis in range(3):
+            if d[axis] == -1:
+                inside = inside * jnp.where(place[axis] > 0, 1, 0)
+            if d[axis] == 1:
+                inside = inside * jnp.where(place[axis] < sizes[axis] - 1, 1, 0)
+        paired = jnp.where((slot >= start) & (slot < start + extent), inside, paired)
+    weight_ref[...] = 1.0 - 0.5 * paired.astype(jnp.float32)
+    loading[2].wait()
+    sign_ref[...] = jnp.broadcast_to(sign_int[...], (loads, order)).astype(jnp.float32)
+    loading[3].wait()
+    spread = jnp.broadcast_to(partner[...], (loads, order))
+    lane_ref[...] = spread & (LANES - 1)
+    tile_ref[...] = jnp.where(paired > 0, spread >> 7, -1)
+
     own_place = pl.ds(
         pl.multiple_of(core * LANES + place[1] * modes_total, modes_total), modes_total
     )
@@ -553,7 +551,7 @@
         coarse_table[:rows_total, :] = leading
         coarse_table[rows_total:, :] = (rows - leading.astype(jnp.float32)).astype(jnp.bfloat16)
 
-    rows_start(0, sizes[0] // 2)
+    rows_start(0, 2)
     modes_near[...] = jnp.zeros_like(modes_near)
     loading[7].wait()
     rows = coarse_own[...]
@@ -586,7 +584,7 @@
                 pieces.append(whole_in[end * sizes[1] + second, :, first * LANES : (first + 1) * LANES])
     coarse = contract_last(jnp.concatenate(pieces, axis=1), own_table[...])
     halo_start(0, local_now + product(coarse, modes_own))
-    rows_start(sizes[0] // 2, sizes[0] * 3 // 4)
+    rows_start(2, 5)
     z_ref[...] = halo_end(0)
 
     def step(number, opening):
@@ -594,14 +592,9 @@
         image = 2 * number + 1
         sign = sign_ref[...]
         conditioned = z_ref[...]
-        parts = in_parts(sign * conditioned)
-        for begin in (0, order // 2):
-            columns = slice(begin, begin + order // 2)
-            mapped_part = jnp.dot(parts, dual[1, :, columns], preferred_element_type=jnp.float32)
-            mapped_part += jnp.dot(parts, dual[0, :, columns], preferred_element_type=jnp.float32)
-            halo_start(image, sign[:, columns] * fold_rows(mapped_part), begin)
+        halo_start(image, sign * product(sign * conditioned, dual))
         if opening:
-            rows_start(sizes[0] * 3 // 4, sizes[0])
+            rows_start(5, sizes[0])
         energy_part = inner(residual[...], conditioned)
         cross_part = inner(conditioned, mapped[...])
         fresh = halo_end(image)

time: 94.5 us -> 93.2 us (0.986)
  Pallas kernels: 91.4 us -> 90.1 us
    pallas_call x1, Pallas kernels: 91.4 us -> 90.1 us  [run(): pl.pallas_call(functools.partial(kernel, sizes), out_shape=jax.ShapeDtype...]
where the time goes in v5:
time: 93.2 us; the launch traced here: 92.8 us
  Pallas kernels  90.1 us (97%)
  local copies, waits for them, and re-layouts  1.4 us (2%)
  between operations  1.29 us (1%)
    pallas_call x1, Pallas kernels, run(): pl.pallas_call(functools.partial(kernel, sizes), out_shape=jax.ShapeDtype...  90.1 us

profile of v5, /device:TPU:1, one launch (start us, length us, event | category | flops | bytes accessed | tf_op | source)
XLA Modules:
  0.0 92.8 jit_solution(14370022956753977765)
XLA Ops:
  1.3 90.1 %shard_map.95 = f32[2,8,1024]{2,1,0:T(8,128)} custom-call(f32[8,1024]{1,0:T(8,128)} %bitcast.17, f32[1024,1024]{1,0:T(8,128)} %bitcast.13, f32[1024,1024]{1,0:T(8,128)} %bitcast.14, f32[32,1024]{1,0:T(8,128)} %bitcast.16, f32[32,8192]{1,0:T(8,128)} %bitcast.15, s32[1,1024]{1,0:T(1,128)} %bitcast.18, s32[1,1024]{1,0:T(1,128)} %bitcast.19, ...), custom_call_target="tpu_custom_call" | custom-call | tf_op jit(solution)/shard_map/pallas_call | solution.py:666
  91.4 1.4 %slice_bitcast_fusion = (f32[1,1,1,8,1024]{4,3,2,1,0:T(8,128)}, f32[1,1,1,8,1024]{4,3,2,1,0:T(8,128)}) fusion(f32[2,8,1024]{2,1,0:T(8,128)} %shard_map.95), kind=kLoop, calls=%fused_computation | loop fusion | bytes 131072 | tf_op jit(solution)/shard_map/reshape;squeeze | solution.py:737
